TPU v7x, 32 devices: a whole 2x2x4 slice. The times are simulated.
32 devices in a mesh: ep: 4 (over y, x), sp: 8 (over z, core).
Axes of the slice: x: 2, y: 2, z: 4, core: 2. Of those that a mesh axis runs over, the one named last changes fastest.
Arguments:
- grad_out: bfloat16 [4096, 4096], P(('ep', 'sp')), may hold values from -1.5 to 1.5
- routes: int32 [4096, 8], P(('ep', 'sp')), may hold values from 0 to 127, as said below
- gate: bfloat16 [4096, 8], P(('ep', 'sp')), may hold values from 0.049804688 to 1
- saved: bfloat16 [4, 8, 64, 3072], P('ep', 'sp'), may hold values from -6 to 6
- w_down: bfloat16 [4, 1536, 4096], P('ep', None, 'sp'), may hold values from -0.15625 to 0.15625
Outputs:
- grad_pre: bfloat16 [4, 8, 64, 3072], P('ep', 'sp')
- grad_gate: float32 [4096, 8], P(('ep', 'sp'))
Inputs may be any that keep to these rules, and one draw needn't show every extreme that they name: `routes`: each row names 8 different experts. In every block of 128 rows at most 16 rows name the same expert whose number is a multiple of 32, and in every block one such expert is named by exactly 16 rows; it is the same expert for all blocks whose indices agree modulo 8.
All inputs are finite; a program needn't handle non-finite values.
Results may differ from a plain program's by a relative error of at most 0.0029.
Values may be sent and summed in bfloat16 or wider, within the bound.
A program may use at most 128 MiB of HBM per device.

v0:
```python
import jax
import jax.numpy as jnp
from jax import lax
from jax.sharding import PartitionSpec as P

EXPERTS = 128


def on_device(grad_out, routes, gate, saved, w_down):
    ep_count = lax.axis_size("ep")
    experts_each = EXPERTS // ep_count
    model_width = grad_out.shape[1]
    slot_count = saved.shape[2]
    capacity = slot_count // ep_count
    hidden_units = saved.shape[3] // 2
    flight = routes % experts_each == 0
    owners = routes // experts_each
    wave_ids = jnp.arange(ep_count, dtype=jnp.int32)
    onehot = (owners[:, :, None] == wave_ids[None, None, :]) & flight[:, :, None]
    member = jnp.sum(onehot.astype(jnp.int32), axis=1)
    gate_by_expert = jnp.sum(
        onehot.astype(jnp.float32) * gate.astype(jnp.float32)[:, :, None], axis=1
    )
    places = jnp.cumsum(member, axis=0) - member
    place_ids = jnp.arange(capacity, dtype=jnp.int32)
    chosen = (places.T[:, None, :] == place_ids[None, :, None]) & (member.T[:, None, :] > 0)
    chosen_float = chosen.astype(jnp.float32)
    outgoing = jnp.einsum(
        "fct,td->fcd", chosen.astype(jnp.bfloat16), grad_out, preferred_element_type=jnp.float32
    ).astype(jnp.bfloat16)
    gate_out = jnp.einsum(
        "fct,tf->fc", chosen_float, gate_by_expert, precision=lax.Precision.HIGHEST
    ).astype(jnp.bfloat16)
    gate_pre = saved[0, 0, :, :hidden_units].astype(jnp.float32)
    up_pre = saved[0, 0, :, hidden_units:].astype(jnp.float32)
    sigmoid_gate = jax.nn.sigmoid(gate_pre)
    silu_gate = gate_pre * sigmoid_gate
    hidden = (silu_gate * up_pre).astype(jnp.bfloat16)
    arrived, gate_in = (
        lax.all_to_all(outgoing, "ep", split_axis=0, concat_axis=0, tiled=True),
        lax.all_to_all(gate_out, "ep", split_axis=0, concat_axis=0, tiled=True),
    )
    arrived = arrived.reshape(slot_count, model_width)
    gate_in = gate_in.reshape(slot_count).astype(jnp.float32)
    grad_hidden = lax.dot_general(
        arrived,
        lax.all_gather(w_down, "sp", axis=2, tiled=True)[0],
        (((1,), (1,)), ((), ())),
        preferred_element_type=jnp.float32,
    )
    score_values = jnp.sum(
        grad_hidden * lax.optimization_barrier(hidden).astype(jnp.float32), axis=1
    )
    scaled = grad_hidden * gate_in[:, None]
    grad_gate_pre = scaled * up_pre * sigmoid_gate * (1.0 + gate_pre * (1.0 - sigmoid_gate))
    grad_up_pre = scaled * silu_gate
    grad_pre = (
        jnp.concatenate([grad_gate_pre, grad_up_pre], axis=1)
        .astype(jnp.bfloat16)
        .reshape(saved.shape)
    )
    returned = lax.all_to_all(
        score_values.reshape(ep_count, capacity), "ep", split_axis=0, concat_axis=0, tiled=True
    )
    score_by_expert = jnp.einsum(
        "fct,fc->tf", chosen_float, returned, precision=lax.Precision.HIGHEST
    )
    grad_gate = jnp.sum(onehot.astype(jnp.float32) * score_by_expert[:, None, :], axis=2)
    return (grad_pre, grad_gate)


def solution(mesh):
    in_specs = (
        P(("ep", "sp"), None),
        P(("ep", "sp"), None),
        P(("ep", "sp"), None),
        P("ep", "sp", None, None),
        P("ep", None, "sp"),
    )
    out_specs = (P("ep", "sp", None, None), P(("ep", "sp"), None))
    return jax.shard_map(
        on_device, mesh=mesh, in_specs=in_specs, out_specs=out_specs, check_vma=False
    )
```

profile of v0, /device:TPU:0, one launch (start us, length us, event | category | flops | bytes accessed | tf_op | source)
XLA Modules:
  0.0 162.5 jit_solution(7661274507109139495)
XLA Ops:
  7.2 0.0 copy-start
  7.2 0.0 copy-start.1
  7.2 0.0 copy-start.2
  7.2 0.0 all-gather.2.cloned.1.call-start
  7.2 0.7 all-gather.2.cloned.1.call-update
  7.9 0.7 fusion.26
  8.6 0.7 add_select_fusion.1
  9.4 0.1 copy.19
  9.5 0.2 reduce_window_sum.11
  9.7 0.1 copy.21
  9.7 0.0 copy-done
  9.7 1.1 convolution_convert_fusion
  10.9 5.2 %all-to-all-start = ((bf16[4,16,4096]{2,1,0:T(8,128)(2,1)}), bf16[4,16,4096]{2,1,0:T(8,128)(2,1)S(1)}, u32[]{:S(2)}, u32[]{:S(2)}) async-start(bf16[4,16,4096]{2,1,0:T(8,128)(2,1)} %convolution_convert_fusion), calls=%async_computation | async-start | bytes 1048576 | tf_op jit(solution)/shard_map/all_to_all | solution.py:40
  16.0 1.1 fusion.6
  17.2 6.9 %all-to-all-done = bf16[4,16,4096]{2,1,0:T(8,128)(2,1)S(1)} async-done(((bf16[4,16,4096]{2,1,0:T(8,128)(2,1)}), bf16[4,16,4096]{2,1,0:T(8,128)(2,1)S(1)}, u32[]{:S(2)}, u32[]{:S(2)}) %all-to-all-start) | async-done | bytes 524320 | tf_op jit(solution)/shard_map/all_to_all | solution.py:40
  24.0 105.1 %all-gather.2.cloned.1.call-done = bf16[1,1536,4096]{2,1,0:T(8,128)(2,1)} async-done(((bf16[1,1536,512]{2,1,0:T(8,128)(2,1)}), bf16[1,1536,4096]{2,1,0:T(8,128)(2,1)}) %all-gather.2.cloned.1.call-update) | async-done | bytes 12582928 | tf_op jit(solution)/shard_map/all_gather | solution.py:47
  129.1 8.6 %multiply_reduce_fusion = (f32[64]{0:T(128)S(1)}, f32[64,1536]{1,0:T(8,128)S(1)}) fusion(bf16[64,1536]{1,0:T(8,128)(2,1)S(1)} %fusion.6, bf16[64,4096]{1,0:T(8,128)(2,1)S(1)} %bitcast.53, bf16[1,1536,4096]{2,1,0:T(8,128)(2,1)} %all-gather.2.cloned.1.call-done), kind=kOutput, calls=%fused_computation.18 | convolution fusion | flops 805601216 | bytes 13697280 | tf_op jit(solution)/shard_map/dot_general | solution.py:45
  137.7 0.7 all_to_all.20
  138.4 3.6 %all-to-all-start.2 = ((f32[4,1,16]{2,1,0:T(1,128)}), f32[4,1,16]{2,1,0:T(1,128)S(1)}, u32[]{:S(2)}, u32[]{:S(2)}) async-start(f32[4,1,16]{2,1,0:T(1,128)} %bitcast.16), calls=%async_computation.2 | async-start | bytes 4096 | tf_op jit(solution)/shard_map/all_to_all | solution.py:62
  142.0 0.0 copy-done.2
  142.0 4.6 %all-to-all-done.2 = f32[4,1,16]{2,1,0:T(1,128)S(1)} async-done(((f32[4,1,16]{2,1,0:T(1,128)}), f32[4,1,16]{2,1,0:T(1,128)S(1)}, u32[]{:S(2)}, u32[]{:S(2)}) %all-to-all-start.2) | async-done | bytes 288 | tf_op jit(solution)/shard_map/all_to_all | solution.py:62
  146.6 0.1 fusion.14
  146.7 0.6 select_reduce_fusion
  147.3 0.1 fusion.16
  147.5 7.0 %all_to_all.26 = bf16[4,1,16]{2,1,0:T(2,128)(2,1)S(1)} all-to-all(bf16[4,1,16]{2,1,0:T(2,128)(2,1)S(1)} %copy.22), channel_id=1, replica_groups=mesh['ep'=4,'sp'=8] {'ep'}, dimensions={0} | all-to-all | bytes 256 | tf_op jit(solution)/shard_map/all_to_all | solution.py:41
  154.5 0.1 reshape.66
  154.6 0.0 copy-done.1
  154.6 0.2 fusion.12
  154.9 0.8 pad_maximum_fusion
  (7 shorter events, 0.1 us)
Async XLA Ops:
  7.2 2.6 %copy-start = (bf16[128,4096]{1,0:T(8,128)(2,1)S(1)}, bf16[128,4096]{1,0:T(8,128)(2,1)}, u32[]{:S(2)}) copy-start(bf16[128,4096]{1,0:T(8,128)(2,1)} %param.5) | copy-start | bytes 3145732
  7.2 147.4 %copy-start.1 = (bf16[1,1,64,3072]{3,2,1,0:T(8,128)(2,1)S(1)}, bf16[1,1,64,3072]{3,2,1,0:T(8,128)(2,1)}, u32[]{:S(2)}) copy-start(bf16[1,1,64,3072]{3,2,1,0:T(8,128)(2,1)} %param.8) | copy-start | bytes 1179652
  7.2 134.8 %copy-start.2 = (bf16[128,8]{0,1:T(8,128)(2,1)S(1)}, bf16[128,8]{0,1:T(8,128)(2,1)}, u32[]{:S(2)}) copy-start(bf16[128,8]{0,1:T(8,128)(2,1)} %param.7) | copy-start | bytes 6148
  7.2 121.9 %all-gather.2.cloned.1.call-start = ((), (), s32[]{:S(2)}) async-start(), calls=%async_computation.3 | async-start | bytes 14155776 | tf_op jit(solution)/shard_map/all_gather | solution.py:47
  10.9 13.2 %all-to-all-start = ((bf16[4,16,4096]{2,1,0:T(8,128)(2,1)}), bf16[4,16,4096]{2,1,0:T(8,128)(2,1)S(1)}, u32[]{:S(2)}, u32[]{:S(2)}) async-start(bf16[4,16,4096]{2,1,0:T(8,128)(2,1)} %convolution_convert_fusion), calls=%async_computation | async-start | bytes 1048576 | tf_op jit(solution)/shard_map/all_to_all | solution.py:40
  138.4 8.2 %all-to-all-start.2 = ((f32[4,1,16]{2,1,0:T(1,128)}), f32[4,1,16]{2,1,0:T(1,128)S(1)}, u32[]{:S(2)}, u32[]{:S(2)}) async-start(f32[4,1,16]{2,1,0:T(1,128)} %bitcast.16), calls=%async_computation.2 | async-start | bytes 4096 | tf_op jit(solution)/shard_map/all_to_all | solution.py:62
Sparse Core Ops, SparseCore 0:
  9.6 119.4 all-gather.1
where the time goes:
time: 163 us; the launch traced here: 162 us
  waiting for transfers between devices  117 us (72%)
  between operations  14.1 us (9%)
  matrix products  10 us (6%)
  starting transfers between devices  8.85 us (5%)
  blocking collectives  6.99 us (4%)
  other arithmetic  4.4 us (3%)
    all_gather x1, waiting for transfers between devices, on_device(): lax.all_gather(w_down, 'sp', axis=2, tiled=True)[0]  105 us
    dot_general x1, matrix products, on_device(): lax.dot_general(arrived, lax.all_gather(w_down, 'sp', axis=2, tiled=True)...  8.6 us
    all_to_all x1, blocking collectives, on_device(): lax.all_to_all(gate_out, 'ep', split_axis=0, concat_axis=0, tiled=True)  6.99 us
    all_to_all x1, waiting for transfers between devices, on_device(): lax.all_to_all(outgoing, 'ep', split_axis=0, concat_axis=0, tiled=True)  6.86 us
    all_to_all x1, starting transfers between devices, on_device(): lax.all_to_all(outgoing, 'ep', split_axis=0, concat_axis=0, tiled=True)  5.17 us
    all_to_all x1, waiting for transfers between devices, on_device(): lax.all_to_all(score_values.reshape(ep_count, capacity), 'ep', split_axis...  4.56 us
    all_to_all x1, starting transfers between devices, on_device(): lax.all_to_all(score_values.reshape(ep_count, capacity), 'ep', split_axis...  3.65 us
  transfers between devices with their start and end apart: 3, of which 3 were waited for; matrix products, arithmetic and copies ran while one was open for 2% of the time, Pallas kernels for 0%

commit v1 on v0

v1 whole, which is shorter than its diff:
```python
import functools

import jax
import jax.numpy as jnp
from jax import lax
from jax.experimental import pallas as pl
from jax.experimental.pallas import tpu as pltpu
from jax.sharding import PartitionSpec as P

EXPERTS = 128
MESH = pl.DeviceIdType.MESH
F32 = jnp.float32
BF16 = jnp.bfloat16


def loop(count, body):
    if count <= 4:
        for i in range(count):
            body(i)
    else:

        @pl.loop(0, count)
        def _(i):
            body(i)


def kernel(
    ep,
    chips,
    routes_ref,
    gate_ref,
    grad_ref,
    saved_ref,
    w_ref,
    pre_ref,
    gg_ref,
    grad_v,
    saved_v,
    wbuf,
    rows_out,
    rows_in,
    gate_out,
    gate_in,
    part_out,
    part_in,
    score_out,
    score_in,
    own,
    hid,
    fa,
    fu,
    pre_v,
    load_sem,
    w_sem,
    row_sem,
    gate_sem,
    part_sem,
    score_sem,
    local_sem,
):
    tokens, top = routes_ref.shape
    cap = rows_out.shape[2]
    cols = rows_out.shape[3]
    slots = ep * cap
    ff = w_ref.shape[0]
    kw = w_ref.shape[1]
    me_e = lax.axis_index("ep")
    me_s = lax.axis_index("sp")
    me_z = me_s // 2
    me_c = me_s % 2
    sibling = me_z * 2 + (1 - me_c)

    load_grad = pltpu.make_async_copy(grad_ref, grad_v, load_sem.at[0])
    load_grad.start()
    load_w = pltpu.make_async_copy(w_ref, wbuf.at[me_c], load_sem.at[1])
    load_w.start()
    load_saved = pltpu.make_async_copy(saved_ref, saved_v, load_sem.at[2])
    load_saved.start()

    barrier = pltpu.get_barrier_semaphore()
    pl.semaphore_signal(barrier, inc=1, device_id=(me_e, sibling), device_id_type=MESH)

    def greet(k):
        e = lax.rem(me_e + k // chips, ep)
        z = lax.rem(me_z + k % chips, chips)
        pl.semaphore_signal(barrier, inc=1, device_id=(e, z * 2 + me_c), device_id_type=MESH)

    @pl.loop(1, ep * chips)
    def _(k):
        greet(k)

    step = EXPERTS // ep
    routes = routes_ref[...]
    gates = gate_ref[...].astype(F32)
    slot_id = lax.broadcasted_iota(jnp.int32, (slots, tokens), 0)
    place_id = (slot_id % cap).astype(F32)
    ones = jnp.ones((cap, top), F32)
    members, weights = [], []
    nt = (((1,), (1,)), ((), ()))
    for f in range(ep):
        hit = (routes == f * step).astype(F32)
        members.append(lax.dot_general(ones, hit, nt, preferred_element_type=F32))
        weights.append(lax.dot_general(ones, hit * gates, nt, preferred_element_type=F32))
    member = jnp.concatenate(members, axis=0)
    weight = jnp.concatenate(weights, axis=0)
    before = (
        lax.broadcasted_iota(jnp.int32, (tokens, tokens), 0)
        < lax.broadcasted_iota(jnp.int32, (tokens, tokens), 1)
    ).astype(F32)
    place = jnp.dot(member.astype(BF16), before.astype(BF16), preferred_element_type=F32)
    chosen = jnp.where((place == place_id) & (member > 0.5), 1.0, 0.0)
    picked = jnp.sum(chosen * weight, axis=1, keepdims=True)
    gate_out[...] = jnp.broadcast_to(picked, (slots, 128)).reshape(ep, cap, 128)
    chosen16 = chosen.astype(BF16)

    load_grad.wait()
    pl.semaphore_wait(barrier, ep * chips)

    w_copy = pltpu.make_async_remote_copy(
        src_ref=w_ref,
        dst_ref=wbuf.at[me_c],
        send_sem=w_sem.at[0],
        recv_sem=w_sem.at[1],
        device_id=(me_e, sibling),
        device_id_type=MESH,
    )
    w_copy.start()

    def row_copy(e, z):
        return pltpu.make_async_remote_copy(
            src_ref=rows_out.at[z, e],
            dst_ref=rows_in.at[me_z, me_e],
            send_sem=row_sem.at[0, z, e],
            recv_sem=row_sem.at[1, me_z, me_e],
            device_id=(e, z * 2 + me_c),
            device_id_type=MESH,
        )

    def row_arrival(e, z):
        return pltpu.make_async_remote_copy(
            src_ref=rows_out.at[me_z, me_e],
            dst_ref=rows_in.at[z, e],
            send_sem=row_sem.at[0, me_z, me_e],
            recv_sem=row_sem.at[1, z, e],
            device_id=(e, z * 2 + me_c),
            device_id_type=MESH,
        )

    def gate_copy(e):
        return pltpu.make_async_remote_copy(
            src_ref=gate_out.at[e],
            dst_ref=gate_in.at[me_e],
            send_sem=gate_sem.at[0, e],
            recv_sem=gate_sem.at[1, me_e],
            device_id=(e, me_s),
            device_id_type=MESH,
        )

    def gate_arrival(e):
        return pltpu.make_async_remote_copy(
            src_ref=gate_out.at[me_e],
            dst_ref=gate_in.at[e],
            send_sem=gate_sem.at[0, me_e],
            recv_sem=gate_sem.at[1, e],
            device_id=(e, me_s),
            device_id_type=MESH,
        )

    def score_copy(e):
        return pltpu.make_async_remote_copy(
            src_ref=score_out.at[e],
            dst_ref=score_in.at[me_e],
            send_sem=score_sem.at[0, e],
            recv_sem=score_sem.at[1, me_e],
            device_id=(e, me_s),
            device_id_type=MESH,
        )

    def score_arrival(e):
        return pltpu.make_async_remote_copy(
            src_ref=score_out.at[me_e],
            dst_ref=score_in.at[e],
            send_sem=score_sem.at[0, me_e],
            recv_sem=score_sem.at[1, e],
            device_id=(e, me_s),
            device_id_type=MESH,
        )

    def part_copy(z):
        return pltpu.make_async_remote_copy(
            src_ref=part_out.at[z],
            dst_ref=part_in.at[me_z],
            send_sem=part_sem.at[0, z],
            recv_sem=part_sem.at[1, me_z],
            device_id=(me_e, z * 2 + me_c),
            device_id_type=MESH,
        )

    def part_arrival(z):
        return pltpu.make_async_remote_copy(
            src_ref=part_out.at[me_z],
            dst_ref=part_in.at[z],
            send_sem=part_sem.at[0, me_z],
            recv_sem=part_sem.at[1, z],
            device_id=(me_e, z * 2 + me_c),
            device_id_type=MESH,
        )

    keep_rows = pltpu.make_async_copy(
        rows_out.at[me_z, me_e], rows_in.at[me_z, me_e], local_sem.at[0]
    )
    keep_gate = pltpu.make_async_copy(gate_out.at[me_e], gate_in.at[me_e], local_sem.at[1])
    keep_score = pltpu.make_async_copy(score_out.at[me_e], score_in.at[me_e], local_sem.at[2])

    def send_rows(i):
        z = lax.rem(me_z + i + 1, chips)
        block = jnp.dot(
            chosen16,
            grad_v[:, pl.ds(pl.multiple_of(z * cols, cols), cols)],
            preferred_element_type=F32,
        )
        rows_out[z] = block.astype(BF16).reshape(ep, cap, cols)

        def one(k):
            e = lax.rem(me_e + k, ep)

            @pl.when((e != me_e) | (z != me_z))
            def _():
                row_copy(e, z).start()

        loop(ep, one)

    loop(chips, send_rows)
    keep_rows.start()
    keep_gate.start()

    @pl.loop(1, ep)
    def _(k):
        gate_copy(lax.rem(me_e + k, ep)).start()

    load_saved.wait()
    block_rows = 16

    @pl.loop(0, slots // block_rows)
    def _(i):
        at = pl.ds(pl.multiple_of(i * block_rows, block_rows), block_rows)
        a = saved_v[at, :ff].astype(F32)
        u = saved_v[at, ff:].astype(F32)
        sig = jax.nn.sigmoid(a)
        silu = a * sig
        hid[at, :] = (silu * u).astype(BF16)
        fa[at, :] = u * sig * (1.0 + a * (1.0 - sig))
        fu[at, :] = silu

    load_w.wait()
    w_copy.wait()

    def times_w(z):
        rows = rows_in[z].reshape(slots, cols)
        return lax.dot_general(
            rows[:, :kw], wbuf[0], nt, preferred_element_type=F32
        ) + lax.dot_general(rows[:, kw:], wbuf[1], nt, preferred_element_type=F32)

    def wait_rows(z):
        def one(k):
            e = lax.rem(me_e + k, ep)

            @pl.when((e != me_e) | (z != me_z))
            def _():
                row_arrival(e, z).wait_recv()

        loop(ep, one)

    def send_part(i):
        z = lax.rem(me_z + chips - 1 - i, chips)
        wait_rows(z)
        part_out[z] = times_w(z).astype(BF16)
        part_copy(z).start()

    loop(chips - 1, send_part)
    wait_rows(me_z)
    keep_rows.wait()
    own[...] = times_w(me_z)

    def add_part(i):
        z = lax.rem(me_z + i + 1, chips)
        part_arrival(z).wait_recv()

        @pl.loop(0, slots // block_rows)
        def _(j):
            at = pl.ds(pl.multiple_of(j * block_rows, block_rows), block_rows)
            own[at, :] += part_in[z, at, :].astype(F32)

    loop(chips - 1, add_part)

    keep_gate.wait()

    @pl.loop(1, ep)
    def _(k):
        gate_arrival(lax.rem(me_e + k, ep)).wait_recv()

    @pl.loop(0, ep)
    def _(e):
        at = pl.ds(pl.multiple_of(e * cap, cap), cap)
        score = jnp.sum(own[at, :] * hid[at, :].astype(F32), axis=1, keepdims=True)
        score_out[e] = jnp.broadcast_to(score, (cap, 128))

    @pl.loop(1, ep)
    def _(k):
        score_copy(lax.rem(me_e + k, ep)).start()

    keep_score.start()

    @pl.loop(0, ep)
    def _(e):
        at = pl.ds(pl.multiple_of(e * cap, cap), cap)
        scaled = own[at, :] * gate_in[e][:, :1]
        pre_v[at, :ff] = (scaled * fa[at, :]).astype(BF16)
        pre_v[at, ff:] = (scaled * fu[at, :]).astype(BF16)

    store = pltpu.make_async_copy(pre_v, pre_ref, load_sem.at[0])
    store.start()

    keep_score.wait()

    @pl.loop(1, ep)
    def _(k):
        score_arrival(lax.rem(me_e + k, ep)).wait_recv()

    got = score_in[...].reshape(slots, 128)
    spread = jnp.sum((chosen * got[:, :1]).reshape(ep, cap, tokens), axis=1)
    pad = -ep % 8
    if pad:
        spread = jnp.concatenate([spread, jnp.zeros((pad, tokens), F32)], axis=0)
    by_token = spread.T
    result = jnp.zeros((tokens, top), F32)
    for f in range(ep):
        result += jnp.where(routes == f * step, by_token[:, f : f + 1], 0.0)
    gg_ref[...] = result

    def sent(k):
        e = lax.rem(me_e + k // chips, ep)
        z = lax.rem(me_z + k % chips, chips)
        row_copy(e, z).wait_send()

    @pl.loop(1, ep * chips)
    def _(k):
        sent(k)

    @pl.loop(1, ep)
    def _(k):
        e = lax.rem(me_e + k, ep)
        gate_copy(e).wait_send()
        score_copy(e).wait_send()

    @pl.loop(1, chips)
    def _(k):
        part_copy(lax.rem(me_z + k, chips)).wait_send()

    store.wait()


def on_device(ep, sp, grad_out, routes, gate, saved, w_down):
    tokens, width = grad_out.shape
    slots = saved.shape[2]
    ff = saved.shape[3] // 2
    kw = w_down.shape[2]
    cap = slots // ep
    chips = sp // 2
    cols = 2 * kw
    vmem = pl.BlockSpec(memory_space=pltpu.VMEM)
    hbm = pl.BlockSpec(memory_space=pl.ANY)
    pre, grad_gate = pl.pallas_call(
        functools.partial(kernel, ep, chips),
        out_shape=(
            jax.ShapeDtypeStruct((slots, 2 * ff), BF16),
            jax.ShapeDtypeStruct((tokens, routes.shape[1]), F32),
        ),
        in_specs=[vmem, vmem, hbm, hbm, hbm],
        out_specs=(hbm, vmem),
        scratch_shapes=[
            pltpu.VMEM((tokens, width), BF16),
            pltpu.VMEM((slots, 2 * ff), BF16),
            pltpu.VMEM((2, ff, kw), BF16),
            pltpu.VMEM((chips, ep, cap, cols), BF16),
            pltpu.VMEM((chips, ep, cap, cols), BF16),
            pltpu.VMEM((ep, cap, 128), F32),
            pltpu.VMEM((ep, cap, 128), F32),
            pltpu.VMEM((chips, slots, ff), BF16),
            pltpu.VMEM((chips, slots, ff), BF16),
            pltpu.VMEM((ep, cap, 128), F32),
            pltpu.VMEM((ep, cap, 128), F32),
            pltpu.VMEM((slots, ff), F32),
            pltpu.VMEM((slots, ff), BF16),
            pltpu.VMEM((slots, ff), F32),
            pltpu.VMEM((slots, ff), F32),
            pltpu.VMEM((slots, 2 * ff), BF16),
            pltpu.SemaphoreType.DMA((3,)),
            pltpu.SemaphoreType.DMA((2,)),
            pltpu.SemaphoreType.DMA((2, chips, ep)),
            pltpu.SemaphoreType.DMA((2, ep)),
            pltpu.SemaphoreType.DMA((2, chips)),
            pltpu.SemaphoreType.DMA((2, ep)),
            pltpu.SemaphoreType.DMA((3,)),
        ],
        compiler_params=pltpu.CompilerParams(
            collective_id=0, has_side_effects=True, vmem_limit_bytes=56 * 1024 * 1024
        ),
    )(routes, gate, grad_out, saved.reshape(slots, 2 * ff), w_down.reshape(ff, kw))
    return pre.reshape(saved.shape), grad_gate


def solution(mesh):
    ep, sp = mesh.shape["ep"], mesh.shape["sp"]
    in_specs = (
        P(("ep", "sp"), None),
        P(("ep", "sp"), None),
        P(("ep", "sp"), None),
        P("ep", "sp", None, None),
        P("ep", None, "sp"),
    )
    out_specs = (P("ep", "sp", None, None), P(("ep", "sp"), None))
    return jax.shard_map(
        functools.partial(on_device, ep, sp),
        mesh=mesh,
        in_specs=in_specs,
        out_specs=out_specs,
        check_vma=False,
    )
```

time: 163 us -> 56.1 us (0.34)
  waiting for transfers between devices: 117 us -> 0 us
  Pallas kernels: 0 us -> 49.1 us
  between operations: 14.1 us -> 0.64 us
  matrix products: 10 us -> 0 us
  starting transfers between devices: 8.85 us -> 0 us
  blocking collectives: 6.99 us -> 0 us
  local copies, waits for them, and re-layouts: 0.97 us -> 6.07 us
  other arithmetic: 4.4 us -> 0 us
    all_gather x1 -> x0, waiting for transfers between devices: 105 us -> none  [on_device(): lax.all_gather(w_down, 'sp', axis=2, tiled=True)[0]]
    pallas_call x0 -> x1, Pallas kernels: none -> 49.1 us  [on_device(): pl.pallas_call(functools.partial(kernel, ep, chips), out_shape=(jax.Shape...]
    all_to_all x2 -> x0, waiting for transfers between devices: 11.4 us -> none  [the longest x1 6.86 us: on_device(): lax.all_to_all(outgoing, 'ep', split_axis=0, concat_axis=0, tiled=True)]
    dot_general x4 -> x0, matrix products: 10 us -> none  [the longest x1 8.6 us: on_device(): lax.dot_general(arrived, lax.all_gather(w_down, 'sp', axis=2, tiled=True)...]
    all_to_all x2 -> x0, starting transfers between devices: 8.81 us -> none  [the longest x1 5.17 us: on_device(): lax.all_to_all(outgoing, 'ep', split_axis=0, concat_axis=0, tiled=True)]
    all_to_all x1 -> x0, blocking collectives: 6.99 us -> none  [on_device(): lax.all_to_all(gate_out, 'ep', split_axis=0, concat_axis=0, tiled=True)]
    unnamed x6 -> x4, local copies, waits for them, and re-layouts: 0.03 us -> 6.07 us
  transfers between devices with their start and end apart: 3 -> 0, of which waited for: 3 -> 0; matrix products, arithmetic and copies ran while one was open for 2% -> 0% of each run, Pallas kernels for 0% -> 0%
where the time goes in v1:
time: 56.1 us; the launch traced here: 55.8 us
  Pallas kernels  49.1 us (88%)
  local copies, waits for them, and re-layouts  6.07 us (11%)
  between operations  0.64 us (1%)
    pallas_call x1, Pallas kernels, on_device(): pl.pallas_call(functools.partial(kernel, ep, chips), out_shape=(jax.Shape...  49.1 us
    unnamed x4, local copies, waits for them, and re-layouts  6.07 us

profile of v1, /device:TPU:0, one launch (start us, length us, event | category | flops | bytes accessed | tf_op | source)
XLA Modules:
  0.0 55.8 jit_solution(16000733710896157421)
XLA Ops:
  0.6 1.4 %copy.8.gate_ref = bf16[128,8]{1,0:T(8,128)(2,1)} copy(bf16[128,8]{0,1:T(8,128)(2,1)} %param.7) | data formatting | bytes 4096 | tf_op args[2]
  2.0 1.4 %copy.7.routes_ref = s32[128,8]{1,0:T(8,128)} copy(s32[128,8]{0,1:T(8,128)} %param.6) | data formatting | bytes 8192 | tf_op args[1]
  3.4 49.1 %shard_map.68 = (bf16[64,3072]{1,0:T(8,128)(2,1)}, f32[128,8]{1,0:T(8,128)}) custom-call(s32[128,8]{1,0:T(8,128)} %copy.7.routes_ref, bf16[128,8]{1,0:T(8,128)(2,1)} %copy.8.gate_ref, bf16[128,4096]{1,0:T(8,128)(2,1)} %grad_ref.1, bf16[64,3072]{1,0:T(8,128)(2,1)} %bitcast.4, bf16[1536,512]{1,0:T(8,128)(2,1)} %bitcast.3), custom_call_target="tpu_custom_call" | custom-call | tf_op jit(solution)/shard_map/pallas_call | solution.py:373
  52.5 1.5 %copy.9 = f32[128,8]{0,1:T(8,128)} copy(f32[128,8]{1,0:T(8,128)} %get-tuple-element.7) | data formatting | bytes 8192
  54.0 1.8 %copy.11 = bf16[1,1,64,3072]{3,2,1,0:T(8,128)(2,1)} copy(bf16[1,1,64,3072]{3,2,1,0:T(8,128)(2,1)} %bitcast.5) | data formatting | bytes 786432

commit v2 on v1

--- a/solution.py
+++ b/solution.py
@@ -58,7 +58,8 @@
     score_sem,
     local_sem,
 ):
-    tokens, top = routes_ref.shape
+    top, tokens = routes_ref.shape
+    nt = (((1,), (1,)), ((), ()))
     cap = rows_out.shape[2]
     cols = rows_out.shape[3]
     slots = ep * cap
@@ -94,13 +95,13 @@
     gates = gate_ref[...].astype(F32)
     slot_id = lax.broadcasted_iota(jnp.int32, (slots, tokens), 0)
     place_id = (slot_id % cap).astype(F32)
-    ones = jnp.ones((cap, top), F32)
     members, weights = [], []
-    nt = (((1,), (1,)), ((), ()))
     for f in range(ep):
         hit = (routes == f * step).astype(F32)
-        members.append(lax.dot_general(ones, hit, nt, preferred_element_type=F32))
-        weights.append(lax.dot_general(ones, hit * gates, nt, preferred_element_type=F32))
+        count = jnp.sum(hit, axis=0, keepdims=True)
+        value = jnp.sum(hit * gates, axis=0, keepdims=True)
+        members.append(jnp.broadcast_to(count, (cap, tokens)))
+        weights.append(jnp.broadcast_to(value, (cap, tokens)))
     member = jnp.concatenate(members, axis=0)
     weight = jnp.concatenate(weights, axis=0)
     before = (
@@ -329,13 +330,9 @@
 
     got = score_in[...].reshape(slots, 128)
     spread = jnp.sum((chosen * got[:, :1]).reshape(ep, cap, tokens), axis=1)
-    pad = -ep % 8
-    if pad:
-        spread = jnp.concatenate([spread, jnp.zeros((pad, tokens), F32)], axis=0)
-    by_token = spread.T
-    result = jnp.zeros((tokens, top), F32)
+    result = jnp.zeros((top, tokens), F32)
     for f in range(ep):
-        result += jnp.where(routes == f * step, by_token[:, f : f + 1], 0.0)
+        result += jnp.where(routes == f * step, spread[f : f + 1, :], 0.0)
     gg_ref[...] = result
 
     def sent(k):
@@ -374,7 +371,7 @@
         functools.partial(kernel, ep, chips),
         out_shape=(
             jax.ShapeDtypeStruct((slots, 2 * ff), BF16),
-            jax.ShapeDtypeStruct((tokens, routes.shape[1]), F32),
+            jax.ShapeDtypeStruct((routes.shape[1], tokens), F32),
         ),
         in_specs=[vmem, vmem, hbm, hbm, hbm],
         out_specs=(hbm, vmem),
@@ -406,8 +403,8 @@
         compiler_params=pltpu.CompilerParams(
             collective_id=0, has_side_effects=True, vmem_limit_bytes=56 * 1024 * 1024
         ),
-    )(routes, gate, grad_out, saved.reshape(slots, 2 * ff), w_down.reshape(ff, kw))
-    return pre.reshape(saved.shape), grad_gate
+    )(routes.T, gate.T, grad_out, saved.reshape(slots, 2 * ff), w_down.reshape(ff, kw))
+    return pre.reshape(saved.shape), grad_gate.T
 
 
 def solution(mesh):

time: 56.1 us -> 52.6 us (0.938)
  local copies, waits for them, and re-layouts: 6.07 us -> 3.03 us
    unnamed x4 -> x2, local copies, waits for them, and re-layouts: 6.07 us -> 3.03 us
where the time goes in v2:
time: 52.6 us; the launch traced here: 52.3 us
  Pallas kernels  48.6 us (92%)
  local copies, waits for them, and re-layouts  3.03 us (6%)
  between operations  0.64 us (1%)
    pallas_call x1, Pallas kernels, on_device(): pl.pallas_call(functools.partial(kernel, ep, chips), out_shape=(jax.Shape...  48.6 us
    unnamed x2, local copies, waits for them, and re-layouts  3.03 us

profile of v2, /device:TPU:0, one launch (start us, length us, event | category | flops | bytes accessed | tf_op | source)
XLA Modules:
  0.0 52.3 jit_solution(1041563531282028695)
XLA Ops:
  0.6 48.6 %shard_map.68 = (bf16[64,3072]{1,0:T(8,128)(2,1)}, f32[8,128]{1,0:T(8,128)}) custom-call(s32[8,128]{1,0:T(8,128)} %bitcast.9, bf16[8,128]{1,0:T(8,128)(2,1)} %bitcast.11, bf16[128,4096]{1,0:T(8,128)(2,1)} %grad_ref.1, bf16[64,3072]{1,0:T(8,128)(2,1)} %bitcast.7, bf16[1536,512]{1,0:T(8,128)(2,1)} %bitcast.6), custom_call_target="tpu_custom_call" | custom-call | tf_op jit(solution)/shard_map/pallas_call | solution.py:370
  49.3 1.8 %copy.9 = bf16[1,1,64,3072]{3,2,1,0:T(8,128)(2,1)} copy(bf16[1,1,64,3072]{3,2,1,0:T(8,128)(2,1)} %bitcast.8) | data formatting | bytes 786432
  51.0 1.3 %copy.10 = f32[128,8]{0,1:T(8,128)} copy(f32[128,8]{0,1:T(8,128)} %bitcast.10) | data formatting | bytes 8192

commit v3 on v2

--- a/solution.py
+++ b/solution.py
@@ -60,6 +60,7 @@
 ):
     top, tokens = routes_ref.shape
     nt = (((1,), (1,)), ((), ()))
+    relayed = chips == 4
     cap = rows_out.shape[2]
     cols = rows_out.shape[3]
     slots = ep * cap
@@ -191,8 +192,8 @@
         return pltpu.make_async_remote_copy(
             src_ref=part_out.at[z],
             dst_ref=part_in.at[me_z],
-            send_sem=part_sem.at[0, z],
-            recv_sem=part_sem.at[1, me_z],
+            send_sem=part_sem.at[0, z, 0],
+            recv_sem=part_sem.at[1, me_z, 0],
             device_id=(me_e, z * 2 + me_c),
             device_id_type=MESH,
         )
@@ -201,8 +202,8 @@
         return pltpu.make_async_remote_copy(
             src_ref=part_out.at[me_z],
             dst_ref=part_in.at[z],
-            send_sem=part_sem.at[0, me_z],
-            recv_sem=part_sem.at[1, z],
+            send_sem=part_sem.at[0, me_z, 0],
+            recv_sem=part_sem.at[1, z, 0],
             device_id=(me_e, z * 2 + me_c),
             device_id_type=MESH,
         )
@@ -213,8 +214,15 @@
     keep_gate = pltpu.make_async_copy(gate_out.at[me_e], gate_in.at[me_e], local_sem.at[1])
     keep_score = pltpu.make_async_copy(score_out.at[me_e], score_in.at[me_e], local_sem.at[2])
 
+    half = me_z // 2
+    partner = me_z + 1 - 2 * (me_z % 2)
+    across = [3 * (1 - half), 2 - half]
+
     def send_rows(i):
-        z = lax.rem(me_z + i + 1, chips)
+        if relayed:
+            z = [*across, partner, me_z][i]
+        else:
+            z = lax.rem(me_z + i + 1, chips)
         block = jnp.dot(
             chosen16,
             grad_v[:, pl.ds(pl.multiple_of(z * cols, cols), cols)],
@@ -272,27 +280,76 @@
 
         loop(ep, one)
 
-    def send_part(i):
-        z = lax.rem(me_z + chips - 1 - i, chips)
-        wait_rows(z)
-        part_out[z] = times_w(z).astype(BF16)
-        part_copy(z).start()
-
-    loop(chips - 1, send_part)
-    wait_rows(me_z)
-    keep_rows.wait()
-    own[...] = times_w(me_z)
-
-    def add_part(i):
-        z = lax.rem(me_z + i + 1, chips)
-        part_arrival(z).wait_recv()
-
-        @pl.loop(0, slots // block_rows)
-        def _(j):
-            at = pl.ds(pl.multiple_of(j * block_rows, block_rows), block_rows)
-            own[at, :] += part_in[z, at, :].astype(F32)
-
-    loop(chips - 1, add_part)
+    piece = slots // 2
+
+    def post(i, j, c, z):
+        at = pl.ds(c * piece, piece)
+        return pltpu.make_async_remote_copy(
+            src_ref=part_out.at[i, at],
+            dst_ref=part_in.at[j, at],
+            send_sem=part_sem.at[0, i, c],
+            recv_sem=part_sem.at[1, j, c],
+            device_id=(me_e, z * 2 + me_c),
+            device_id_type=MESH,
+        )
+
+    def relay_parts():
+        edge = me_z % 3 == 0
+        for i in range(2):
+            wait_rows(across[i])
+            own[...] = times_w(across[i])
+            for c in range(2):
+                at = pl.ds(c * piece, piece)
+
+                @pl.when(edge)
+                def _():
+                    part_out[i, at, :] = own[at, :].astype(BF16)
+                    post(i, 2 + i, c, partner).start()
+
+                @pl.when(jnp.logical_not(edge))
+                def _():
+                    post(i, 2 + i, c, partner).wait_recv()
+                    total = own[at, :] + part_in[2 + i, at, :].astype(F32)
+                    part_out[i, at, :] = total.astype(BF16)
+                    post(i, 1, c, across[i]).start()
+
+        wait_rows(partner)
+        part_out[2] = times_w(partner).astype(BF16)
+        for c in range(2):
+            post(2, 0, c, partner).start()
+        wait_rows(me_z)
+        keep_rows.wait()
+        own[...] = times_w(me_z)
+        for j in range(2):
+            for c in range(2):
+                at = pl.ds(c * piece, piece)
+                post(2, j, c, partner).wait_recv()
+                own[at, :] += part_in[j, at, :].astype(F32)
+
+    if relayed:
+        relay_parts()
+    else:
+        def send_part(i):
+            z = lax.rem(me_z + chips - 1 - i, chips)
+            wait_rows(z)
+            part_out[z] = times_w(z).astype(BF16)
+            part_copy(z).start()
+
+        loop(chips - 1, send_part)
+        wait_rows(me_z)
+        keep_rows.wait()
+        own[...] = times_w(me_z)
+
+        def add_part(i):
+            z = lax.rem(me_z + i + 1, chips)
+            part_arrival(z).wait_recv()
+
+            @pl.loop(0, slots // block_rows)
+            def _(j):
+                at = pl.ds(pl.multiple_of(j * block_rows, block_rows), block_rows)
+                own[at, :] += part_in[z, at, :].astype(F32)
+
+        loop(chips - 1, add_part)
 
     keep_gate.wait()
 
@@ -350,9 +407,15 @@
         gate_copy(e).wait_send()
         score_copy(e).wait_send()
 
-    @pl.loop(1, chips)
-    def _(k):
-        part_copy(lax.rem(me_z + k, chips)).wait_send()
+    if relayed:
+        for i in range(3):
+            for c in range(2):
+                post(i, 0, c, partner).wait_send()
+    else:
+
+        @pl.loop(1, chips)
+        def _(k):
+            part_copy(lax.rem(me_z + k, chips)).wait_send()
 
     store.wait()
 
@@ -396,7 +459,7 @@
             pltpu.SemaphoreType.DMA((2,)),
             pltpu.SemaphoreType.DMA((2, chips, ep)),
             pltpu.SemaphoreType.DMA((2, ep)),
-            pltpu.SemaphoreType.DMA((2, chips)),
+            pltpu.SemaphoreType.DMA((2, chips, 2)),
             pltpu.SemaphoreType.DMA((2, ep)),
             pltpu.SemaphoreType.DMA((3,)),
         ],

time: 52.6 us -> 41.2 us (0.78)
  Pallas kernels: 48.6 us -> 37.3 us
    pallas_call x1, Pallas kernels: 48.6 us -> 37.3 us  [on_device(): pl.pallas_call(functools.partial(kernel, ep, chips), out_shape=(jax.Shape...]
where the time goes in v3:
time: 41.2 us; the launch traced here: 41 us
  Pallas kernels  37.3 us (91%)
  local copies, waits for them, and re-layouts  3.03 us (7%)
  between operations  0.64 us (2%)
    pallas_call x1, Pallas kernels, on_device(): pl.pallas_call(functools.partial(kernel, ep, chips), out_shape=(jax.Shape...  37.3 us
    unnamed x2, local copies, waits for them, and re-layouts  3.03 us

profile of v3, /device:TPU:0, one launch (start us, length us, event | category | flops | bytes accessed | tf_op | source)
XLA Modules:
  0.0 41.0 jit_solution(9343944628736248104)
XLA Ops:
  0.6 37.3 %shard_map.68 = (bf16[64,3072]{1,0:T(8,128)(2,1)}, f32[8,128]{1,0:T(8,128)}) custom-call(s32[8,128]{1,0:T(8,128)} %bitcast.9, bf16[8,128]{1,0:T(8,128)(2,1)} %bitcast.11, bf16[128,4096]{1,0:T(8,128)(2,1)} %grad_ref.1, bf16[64,3072]{1,0:T(8,128)(2,1)} %bitcast.7, bf16[1536,512]{1,0:T(8,128)(2,1)} %bitcast.6), custom_call_target="tpu_custom_call" | custom-call | tf_op jit(solution)/shard_map/pallas_call | solution.py:433
  37.9 1.8 %copy.9 = bf16[1,1,64,3072]{3,2,1,0:T(8,128)(2,1)} copy(bf16[1,1,64,3072]{3,2,1,0:T(8,128)(2,1)} %bitcast.8) | data formatting | bytes 786432
  39.7 1.3 %copy.10 = f32[128,8]{0,1:T(8,128)} copy(f32[128,8]{0,1:T(8,128)} %bitcast.10) | data formatting | bytes 8192

commit v4 on v3

--- a/solution.py
+++ b/solution.py
@@ -126,7 +126,6 @@
         device_id=(me_e, sibling),
         device_id_type=MESH,
     )
-    w_copy.start()
 
     def row_copy(e, z):
         return pltpu.make_async_remote_copy(
@@ -240,6 +239,7 @@
         loop(ep, one)
 
     loop(chips, send_rows)
+    w_copy.start()
     keep_rows.start()
     keep_gate.start()
 
@@ -280,7 +280,7 @@
 
         loop(ep, one)
 
-    piece = slots // 2
+    piece = slots // 4
 
     def post(i, j, c, z):
         at = pl.ds(c * piece, piece)
@@ -295,10 +295,18 @@
 
     def relay_parts():
         edge = me_z % 3 == 0
+
+        def send_partner():
+            wait_rows(partner)
+            part_out[2] = times_w(partner).astype(BF16)
+            for c in range(4):
+                post(2, 0, c, partner).start()
+
+        pl.when(jnp.logical_not(edge))(send_partner)
         for i in range(2):
             wait_rows(across[i])
             own[...] = times_w(across[i])
-            for c in range(2):
+            for c in range(4):
                 at = pl.ds(c * piece, piece)
 
                 @pl.when(edge)
@@ -313,15 +321,12 @@
                     part_out[i, at, :] = total.astype(BF16)
                     post(i, 1, c, across[i]).start()
 
-        wait_rows(partner)
-        part_out[2] = times_w(partner).astype(BF16)
-        for c in range(2):
-            post(2, 0, c, partner).start()
+        pl.when(edge)(send_partner)
         wait_rows(me_z)
         keep_rows.wait()
         own[...] = times_w(me_z)
         for j in range(2):
-            for c in range(2):
+            for c in range(4):
                 at = pl.ds(c * piece, piece)
                 post(2, j, c, partner).wait_recv()
                 own[at, :] += part_in[j, at, :].astype(F32)
@@ -409,7 +414,7 @@
 
     if relayed:
         for i in range(3):
-            for c in range(2):
+            for c in range(4):
                 post(i, 0, c, partner).wait_send()
     else:
 
@@ -459,7 +464,7 @@
             pltpu.SemaphoreType.DMA((2,)),
             pltpu.SemaphoreType.DMA((2, chips, ep)),
             pltpu.SemaphoreType.DMA((2, ep)),
-            pltpu.SemaphoreType.DMA((2, chips, 2)),
+            pltpu.SemaphoreType.DMA((2, chips, 4)),
             pltpu.SemaphoreType.DMA((2, ep)),
             pltpu.SemaphoreType.DMA((3,)),
         ],

time: 41.2 us -> 38 us (0.922)
  Pallas kernels: 37.3 us -> 34.1 us
    pallas_call x1, Pallas kernels: 37.3 us -> 34.1 us  [on_device(): pl.pallas_call(functools.partial(kernel, ep, chips), out_shape=(jax.Shape...]
where the time goes in v4:
time: 38 us; the launch traced here: 37.8 us
  Pallas kernels  34.1 us (90%)
  local copies, waits for them, and re-layouts  3.03 us (8%)
  between operations  0.64 us (2%)
    pallas_call x1, Pallas kernels, on_device(): pl.pallas_call(functools.partial(kernel, ep, chips), out_shape=(jax.Shape...  34.1 us
    unnamed x2, local copies, waits for them, and re-layouts  3.03 us

profile of v4, /device:TPU:0, one launch (start us, length us, event | category | flops | bytes accessed | tf_op | source)
XLA Modules:
  0.0 37.8 jit_solution(10231856073845481593)
XLA Ops:
  0.6 34.1 %shard_map.68 = (bf16[64,3072]{1,0:T(8,128)(2,1)}, f32[8,128]{1,0:T(8,128)}) custom-call(s32[8,128]{1,0:T(8,128)} %bitcast.9, bf16[8,128]{1,0:T(8,128)(2,1)} %bitcast.11, bf16[128,4096]{1,0:T(8,128)(2,1)} %grad_ref.1, bf16[64,3072]{1,0:T(8,128)(2,1)} %bitcast.7, bf16[1536,512]{1,0:T(8,128)(2,1)} %bitcast.6), custom_call_target="tpu_custom_call" | custom-call | tf_op jit(solution)/shard_map/pallas_call | solution.py:438
  34.7 1.8 %copy.9 = bf16[1,1,64,3072]{3,2,1,0:T(8,128)(2,1)} copy(bf16[1,1,64,3072]{3,2,1,0:T(8,128)(2,1)} %bitcast.8) | data formatting | bytes 786432
  36.5 1.3 %copy.10 = f32[128,8]{0,1:T(8,128)} copy(f32[128,8]{0,1:T(8,128)} %bitcast.10) | data formatting | bytes 8192

commit v5 on v4

--- a/solution.py
+++ b/solution.py
@@ -46,6 +46,7 @@
     score_out,
     score_in,
     own,
+    tmp,
     hid,
     fa,
     fu,
@@ -302,29 +303,30 @@
             for c in range(4):
                 post(2, 0, c, partner).start()
 
+            wait_rows(me_z)
+            keep_rows.wait()
+            own[...] = times_w(me_z)
+
         pl.when(jnp.logical_not(edge))(send_partner)
         for i in range(2):
             wait_rows(across[i])
-            own[...] = times_w(across[i])
+            tmp[...] = times_w(across[i])
             for c in range(4):
                 at = pl.ds(c * piece, piece)
 
                 @pl.when(edge)
                 def _():
-                    part_out[i, at, :] = own[at, :].astype(BF16)
+                    part_out[i, at, :] = tmp[at, :].astype(BF16)
                     post(i, 2 + i, c, partner).start()
 
                 @pl.when(jnp.logical_not(edge))
                 def _():
                     post(i, 2 + i, c, partner).wait_recv()
-                    total = own[at, :] + part_in[2 + i, at, :].astype(F32)
+                    total = tmp[at, :] + part_in[2 + i, at, :].astype(F32)
                     part_out[i, at, :] = total.astype(BF16)
                     post(i, 1, c, across[i]).start()
 
         pl.when(edge)(send_partner)
-        wait_rows(me_z)
-        keep_rows.wait()
-        own[...] = times_w(me_z)
         for j in range(2):
             for c in range(4):
                 at = pl.ds(c * piece, piece)
@@ -456,6 +458,7 @@
             pltpu.VMEM((ep, cap, 128), F32),
             pltpu.VMEM((ep, cap, 128), F32),
             pltpu.VMEM((slots, ff), F32),
+            pltpu.VMEM((slots, ff), F32),
             pltpu.VMEM((slots, ff), BF16),
             pltpu.VMEM((slots, ff), F32),
             pltpu.VMEM((slots, ff), F32),

time: 38 us -> 38 us (level)
  no operation moved by 1% of the time
where the time goes in v5:
time: 38 us; the launch traced here: 37.8 us
  Pallas kernels  34.1 us (90%)
  local copies, waits for them, and re-layouts  3.03 us (8%)
  between operations  0.64 us (2%)
    pallas_call x1, Pallas kernels, on_device(): pl.pallas_call(functools.partial(kernel, ep, chips), out_shape=(jax.Shape...  34.1 us
    unnamed x2, local copies, waits for them, and re-layouts  3.03 us

profile of v5, /device:TPU:0, one launch (start us, length us, event | category | flops | bytes accessed | tf_op | source)
XLA Modules:
  0.0 37.8 jit_solution(13068218630268875486)
XLA Ops:
  0.6 34.1 %shard_map.68 = (bf16[64,3072]{1,0:T(8,128)(2,1)}, f32[8,128]{1,0:T(8,128)}) custom-call(s32[8,128]{1,0:T(8,128)} %bitcast.9, bf16[8,128]{1,0:T(8,128)(2,1)} %bitcast.11, bf16[128,4096]{1,0:T(8,128)(2,1)} %grad_ref.1, bf16[64,3072]{1,0:T(8,128)(2,1)} %bitcast.7, bf16[1536,512]{1,0:T(8,128)(2,1)} %bitcast.6), custom_call_target="tpu_custom_call" | custom-call | tf_op jit(solution)/shard_map/pallas_call | solution.py:440
  34.7 1.8 %copy.9 = bf16[1,1,64,3072]{3,2,1,0:T(8,128)(2,1)} copy(bf16[1,1,64,3072]{3,2,1,0:T(8,128)(2,1)} %bitcast.8) | data formatting | bytes 786432
  36.5 1.3 %copy.10 = f32[128,8]{0,1:T(8,128)} copy(f32[128,8]{0,1:T(8,128)} %bitcast.10) | data formatting | bytes 8192

commit v6 on v4

--- a/solution.py
+++ b/solution.py
@@ -325,11 +325,21 @@
         wait_rows(me_z)
         keep_rows.wait()
         own[...] = times_w(me_z)
-        for j in range(2):
-            for c in range(4):
-                at = pl.ds(c * piece, piece)
-                post(2, j, c, partner).wait_recv()
-                own[at, :] += part_in[j, at, :].astype(F32)
+        for c in range(4):
+            at = pl.ds(c * piece, piece)
+            post(2, 0, c, partner).wait_recv()
+            post(2, 1, c, partner).wait_recv()
+            total = own[at, :] + part_in[0, at, :].astype(F32)
+            total += part_in[1, at, :].astype(F32)
+            own[at, :] = total
+            if piece == cap:
+                score = jnp.sum(total * hid[at, :].astype(F32), axis=1, keepdims=True)
+                score_out[c] = jnp.broadcast_to(score, (cap, 128))
+
+                @pl.when(c != me_e)
+                def _():
+                    score_copy(c).start()
+
 
     if relayed:
         relay_parts()
@@ -362,15 +372,17 @@
     def _(k):
         gate_arrival(lax.rem(me_e + k, ep)).wait_recv()
 
-    @pl.loop(0, ep)
-    def _(e):
-        at = pl.ds(pl.multiple_of(e * cap, cap), cap)
-        score = jnp.sum(own[at, :] * hid[at, :].astype(F32), axis=1, keepdims=True)
-        score_out[e] = jnp.broadcast_to(score, (cap, 128))
-
-    @pl.loop(1, ep)
-    def _(k):
-        score_copy(lax.rem(me_e + k, ep)).start()
+    if not (relayed and slots // 4 == cap):
+
+        @pl.loop(0, ep)
+        def _(e):
+            at = pl.ds(pl.multiple_of(e * cap, cap), cap)
+            score = jnp.sum(own[at, :] * hid[at, :].astype(F32), axis=1, keepdims=True)
+            score_out[e] = jnp.broadcast_to(score, (cap, 128))
+
+        @pl.loop(1, ep)
+        def _(k):
+            score_copy(lax.rem(me_e + k, ep)).start()
 
     keep_score.start()
 

time: 38 us -> 36.3 us (0.955)
  the two profiles are of different devices: /device:TPU:0 before, /device:TPU:14 now
where the time goes in v6:
time: 36.3 us; the launch traced here: 36 us
  Pallas kernels  32.4 us (89%)
  local copies, waits for them, and re-layouts  3.03 us (8%)
  between operations  0.64 us (2%)
    pallas_call x1, Pallas kernels, on_device(): pl.pallas_call(functools.partial(kernel, ep, chips), out_shape=(jax.Shape...  32.4 us
    unnamed x2, local copies, waits for them, and re-layouts  3.03 us

profile of v6, /device:TPU:14, one launch (start us, length us, event | category | flops | bytes accessed | tf_op | source)
XLA Modules:
  0.0 36.0 jit_solution(9282287801455477312)
XLA Ops:
  0.6 32.4 %shard_map.68 = (bf16[64,3072]{1,0:T(8,128)(2,1)}, f32[8,128]{1,0:T(8,128)}) custom-call(s32[8,128]{1,0:T(8,128)} %bitcast.9, bf16[8,128]{1,0:T(8,128)(2,1)} %bitcast.11, bf16[128,4096]{1,0:T(8,128)(2,1)} %grad_ref.1, bf16[64,3072]{1,0:T(8,128)(2,1)} %bitcast.7, bf16[1536,512]{1,0:T(8,128)(2,1)} %bitcast.6), custom_call_target="tpu_custom_call" | custom-call | tf_op jit(solution)/shard_map/pallas_call | solution.py:450
  33.0 1.8 %copy.9 = bf16[1,1,64,3072]{3,2,1,0:T(8,128)(2,1)} copy(bf16[1,1,64,3072]{3,2,1,0:T(8,128)(2,1)} %bitcast.8) | data formatting | bytes 786432
  34.8 1.3 %copy.10 = f32[128,8]{0,1:T(8,128)} copy(f32[128,8]{0,1:T(8,128)} %bitcast.10) | data formatting | bytes 8192
